TPU v7x, 32 devices: a whole 2x2x4 slice. The times are simulated.
32 devices in a mesh: groups: 2 (over y), row: 4 (over z), col: 2 (over x), sub: 2 (over core).
Axes of the slice: x: 2, y: 2, z: 4, core: 2. Of those that a mesh axis runs over, the one named last changes fastest.
Arguments:
- alignment: bfloat16 [64, 128, 256], P(('groups', 'row', 'col')), parts along dimension 0, may hold values from -12 to 12, as said below
- alignment_mask: int32 [64, 128], P(('groups', 'row', 'col')), parts along dimension 0, may hold values from 0 to 1
- residue_mask: int32 [256], P('groups'), parts along dimension 0, may hold values 0 or 1
- pair_state: bfloat16 [256, 128, 128], P(('groups', 'row'), ('col', 'sub')), parts along dimension 0, may hold values from -8 to 8
- alignment_gain: float32 [256], replicated, may hold values from 0.1 to 1.9
- alignment_offset: float32 [256], replicated, may hold values from -3 to 3
- left_weight: bfloat16 [256, 32], replicated, may hold values from -0.375 to 0.375
- left_offset: float32 [32], replicated, may hold values from -3 to 3
- right_weight: bfloat16 [256, 32], replicated, may hold values from -0.375 to 0.375
- right_offset: float32 [32], replicated, may hold values from -3 to 3
- out_weight: bfloat16 [32, 32, 128], replicated, may hold values from -0.1875 to 0.1875
- out_offset: float32 [128], replicated, may hold values from -3 to 3
- pair_gain: float32 [128], replicated, may hold values from 0.1 to 1.9
- pair_offset: float32 [128], replicated, may hold values from -3 to 3
Outputs:
- new_pair: bfloat16 [256, 128, 128], P(('groups', 'row'), ('col', 'sub')), parts along dimension 0
There are 2 independent parts, one for each index of `groups`. A program takes and returns all parts, laid end to end along the dimension named above; an argument that names none is the same for every part. Nothing has to cross between parts.
Inputs may be any that keep to these rules, and one draw needn't show every extreme that they name: `alignment`: whole rows of the representation, with spread channel scales.
All inputs are finite; a program needn't handle non-finite values.
Results may differ from a plain program's by a relative error of at most 0.0053.
Values may be sent and summed in bfloat16 or wider, within the bound.
A program may use at most 128 MiB of HBM per device.

v0:
```python
import jax
import jax.numpy as jnp
from jax import lax
from jax.sharding import PartitionSpec as P


def normalize(values, scales, offsets):
    average = jnp.mean(values, axis=-1, keepdims=True)
    variance = jnp.mean(values * values, axis=-1, keepdims=True) - average * average
    return (values - average) * lax.rsqrt(variance + 1e-05) * scales + offsets


def project_side(normed, weight, offsets, factor):
    leading = normed.shape[:-1]
    flattened = jnp.dot(
        normed.reshape(-1, normed.shape[-1]), weight, preferred_element_type=jnp.float32
    )
    return ((flattened.reshape(leading + (weight.shape[1],)) + offsets) * factor[..., None]).astype(
        jnp.bfloat16
    )


def reorder(values, row_count, col_count, sub_count):
    local_seqs = values.shape[0]
    portion = values.shape[1] // (row_count * col_count * sub_count)
    trailing = values.shape[2:]
    grouped = values.reshape((local_seqs, col_count, sub_count, row_count, portion) + trailing)
    extra = tuple(range(5, 5 + len(trailing)))
    return jnp.transpose(grouped, (0, 3, 1, 2, 4) + extra).reshape(values.shape)


def own_half(values, sub_count, sub_index):
    sequences = values.shape[0]
    share = values.shape[1] // sub_count
    split = values.reshape((sequences, sub_count, share) + values.shape[2:])
    picked = lax.dynamic_slice_in_dim(split, sub_index, 1, 1)
    return picked.reshape((sequences, share) + values.shape[2:])


def column_terms(left_rows, row_mask, right_cols, col_mask, out_flat, out_offset):
    col_total = right_cols.shape[1]
    results = []
    for first_col in range(0, col_total, 32):
        last_col = min(first_col + 32, col_total)
        selected = right_cols[:, first_col:last_col]
        products = jnp.einsum(
            "sic,sje->ijce", left_rows, selected, preferred_element_type=jnp.float32
        ).astype(jnp.bfloat16)
        pair_rows = products.shape[0] * products.shape[1]
        projected = jnp.dot(
            products.reshape(pair_rows, -1), out_flat, preferred_element_type=jnp.float32
        )
        projected = projected.reshape(products.shape[0], products.shape[1], -1) + out_offset
        counts = jnp.dot(
            row_mask.T, col_mask[:, first_col:last_col], preferred_element_type=jnp.float32
        )
        results.append(projected / jnp.maximum(counts, 1.0)[:, :, None])
    return jnp.concatenate(results, axis=1)


def body(
    alignment,
    alignment_mask,
    residue_mask,
    pair_state,
    alignment_gain,
    alignment_offset,
    left_weight,
    left_offset,
    right_weight,
    right_offset,
    out_weight,
    out_offset,
    pair_gain,
    pair_offset,
):
    row_count = lax.axis_size("row")
    col_count = lax.axis_size("col")
    sub_count = lax.axis_size("sub")
    sub_index = lax.axis_index("sub")
    local_seqs, residues, channels = alignment.shape
    hidden = left_weight.shape[1]
    portion = residues // (row_count * col_count)
    present = (alignment_mask * residue_mask[None, :]).astype(jnp.bfloat16)
    normed = normalize(alignment.astype(jnp.float32), alignment_gain, alignment_offset).astype(
        jnp.bfloat16
    )
    factor = present.astype(jnp.float32)
    left_local = project_side(normed, left_weight, left_offset, factor)
    right_local = reorder(
        project_side(normed, right_weight, right_offset, factor), row_count, col_count, sub_count
    )
    outgoing = (
        left_local.reshape(local_seqs, -1),
        right_local.reshape(local_seqs, -1),
        present,
        reorder(present, row_count, col_count, sub_count),
    )
    arrived = (
        lax.all_to_all(outgoing[0], ("row", "col"), split_axis=1, concat_axis=0, tiled=True),
        lax.all_to_all(outgoing[1], ("row", "col"), split_axis=1, concat_axis=0, tiled=True),
        lax.all_to_all(outgoing[2], ("row", "col"), split_axis=1, concat_axis=0, tiled=True),
        lax.all_to_all(outgoing[3], ("row", "col"), split_axis=1, concat_axis=0, tiled=True),
    )
    sequences = arrived[2].shape[0]
    left_part = arrived[0].reshape(sequences, portion, hidden)
    right_part = own_half(arrived[1].reshape(sequences, portion, hidden), sub_count, sub_index)
    mask_here = arrived[2]
    mask_there = own_half(arrived[3], sub_count, sub_index)
    gathered_rows, row_mask = (
        lax.all_gather(left_part.reshape(sequences, -1), "col", axis=1, tiled=True),
        lax.all_gather(mask_here, "col", axis=1, tiled=True),
    )
    left_rows = gathered_rows.reshape(sequences, -1, hidden)
    out_flat = out_weight.reshape(hidden * hidden, -1)
    pieces = lax.all_gather((right_part, mask_there), "row", axis=1, tiled=True)
    update = column_terms(left_rows, row_mask, pieces[0], pieces[1], out_flat, out_offset)
    summed = pair_state.astype(jnp.float32) + update
    return normalize(summed, pair_gain, pair_offset).astype(jnp.bfloat16)


def solution(mesh):
    placed = (
        P(("groups", "row", "col"), None, None),
        P(("groups", "row", "col"), None),
        P("groups"),
        P(("groups", "row"), ("col", "sub"), None),
        P(),
        P(),
        P(),
        P(),
        P(),
        P(),
        P(),
        P(),
        P(),
        P(),
    )
    return jax.shard_map(
        body,
        mesh=mesh,
        in_specs=placed,
        out_specs=P(("groups", "row"), ("col", "sub"), None),
        check_vma=False,
    )
```

profile of v0, /device:TPU:0, one launch (start us, length us, event | category | flops | bytes accessed | tf_op | source)
XLA Modules:
  0.0 94.4 jit_solution(10533746370622199730)
XLA Ops:
  0.0 0.7 fusion.22
  0.9 0.6 copy.62
  1.5 7.3 %all-to-all-start.3 = ((bf16[4,8,16]{2,0,1:T(4,128)(2,1)}), bf16[4,8,16]{2,0,1:T(4,128)(2,1)S(1)}, u32[]{:S(2)}, u32[]{:S(2)}) async-start(bf16[4,8,16]{2,0,1:T(4,128)(2,1)} %copy.62), calls=%async_computation.3 | async-start | bytes 16384 | tf_op jit(solution)/shard_map/all_to_all | solution.py:103
  8.8 1.2 %convert_reduce_fusion = (f32[4,128]{1,0:T(4,128)S(1)}, f32[4,128]{1,0:T(4,128)S(1)}) fusion(bf16[4,128,256]{2,1,0:T(8,128)(2,1)} %param.14), kind=kLoop, calls=%fused_computation.14 | loop fusion | flops 523264 | bytes 266240 | tf_op jit(solution)/shard_map/reduce_sum | solution.py:8
  10.0 1.3 %fusion.6 = bf16[4,128,32]{1,2,0:T(8,128)(2,1)S(1)} fusion(bf16[4,128,256]{2,1,0:T(8,128)(2,1)} %param.14, f32[256]{0:T(256)} %param.19, f32[256]{0:T(256)} %param.18, f32[4,128]{1,0:T(4,128)S(1)} %get-tuple-element.14, f32[4,128]{1,0:T(4,128)S(1)} %get-tuple-element.13, f32[4,128]{1,0:T(4,128)S(1)} %get-tuple-element.9, f32[32]{0:T(128)} %param.23, ...), kind=kOutput, calls=%fused_computation.10 | convolution fusion | flops 9224192 | bytes 319616 | tf_op jit(solution)/shard_map/dot_general | solution.py:15
  11.3 1.3 %fusion.5 = bf16[4,128,32]{1,2,0:T(8,128)(2,1)S(1)} fusion(bf16[4,128,256]{2,1,0:T(8,128)(2,1)} %param.14, f32[256]{0:T(256)} %param.19, f32[256]{0:T(256)} %param.18, f32[4,128]{1,0:T(4,128)S(1)} %get-tuple-element.14, f32[4,128]{1,0:T(4,128)S(1)} %get-tuple-element.13, f32[32]{0:T(128)} %param.21, f32[4,128]{1,0:T(4,128)S(1)} %get-tuple-element.9, ...), kind=kOutput, calls=%fused_computation.9 | convolution fusion | flops 9224192 | bytes 319616 | tf_op jit(solution)/shard_map/dot_general | solution.py:15
  12.7 0.1 copy.50
  12.9 0.8 reshape.110
  13.8 0.2 all_to_all.55
  14.0 0.6 copy.56
  14.6 0.6 copy.59
  15.3 5.9 %all-to-all-start.2 = ((bf16[4,8,16]{2,0,1:T(4,128)(2,1)}), bf16[4,8,16]{2,0,1:T(4,128)(2,1)S(1)}, u32[]{:S(2)}, u32[]{:S(2)}) async-start(bf16[4,8,16]{2,0,1:T(4,128)(2,1)} %copy.59), calls=%async_computation.2 | async-start | bytes 16384 | tf_op jit(solution)/shard_map/all_to_all | solution.py:102
  21.4 12.4 %all-gather.1 = bf16[32,1,32]{0,2,1:T(8,128)(2,1)S(1)} all-gather(bf16[32,1,8]{0,2,1:T(8,128)(2,1)S(1)} %copy.63), channel_id=3, replica_groups=mesh['groups'=2,'row'=4,'col'=2,'sub'=2] {'row'}, dimensions={2}, use_global_device_ids=true | all-gather | bytes 2560 | tf_op jit(solution)/shard_map/all_gather | solution.py:116
  33.8 4.2 %all-to-all-start = ((bf16[4,8,512]{2,0,1:T(4,128)(2,1)}), bf16[4,8,512]{2,0,1:T(4,128)(2,1)S(1)}, u32[]{:S(2)}, u32[]{:S(2)}) async-start(bf16[4,8,512]{2,0,1:T(4,128)(2,1)} %reshape.110), calls=%async_computation | async-start | bytes 65536 | tf_op jit(solution)/shard_map/all_to_all | solution.py:101
  38.1 4.3 %all_gather.14 = bf16[32,32]{0,1:T(8,128)(2,1)S(1)} all-gather(bf16[32,16]{0,1:T(8,128)(2,1)S(1)} %copy.60), channel_id=1, replica_groups=mesh['groups'=2,'row'=4,'col'=2,'sub'=2] {'col'}, dimensions={1}, use_global_device_ids=true | all-gather | bytes 3072 | tf_op jit(solution)/shard_map/all_gather | solution.py:112
  42.5 2.2 %all-to-all-done = bf16[4,8,512]{2,0,1:T(4,128)(2,1)S(1)} async-done(((bf16[4,8,512]{2,0,1:T(4,128)(2,1)}), bf16[4,8,512]{2,0,1:T(4,128)(2,1)S(1)}, u32[]{:S(2)}, u32[]{:S(2)}) %all-to-all-start) | async-done | bytes 32800 | tf_op jit(solution)/shard_map/all_to_all | solution.py:101
  44.7 3.9 %all-to-all-start.1 = ((bf16[4,8,512]{2,0,1:T(4,128)(2,1)}), bf16[4,8,512]{2,0,1:T(4,128)(2,1)S(1)}, u32[]{:S(2)}, u32[]{:S(2)}) async-start(bf16[4,8,512]{2,0,1:T(4,128)(2,1)} %copy.56), calls=%async_computation.1 | async-start | bytes 65536 | tf_op jit(solution)/shard_map/all_to_all | solution.py:100
  48.7 14.3 %all-gather = bf16[32,1,32,32]{3,0,1,2:T(8,128)(2,1)S(1)} all-gather(bf16[32,1,8,32]{3,0,1,2:T(8,128)(2,1)S(1)} %copy.53), channel_id=2, replica_groups=mesh['groups'=2,'row'=4,'col'=2,'sub'=2] {'row'}, dimensions={2}, use_global_device_ids=true | all-gather | bytes 81920 | tf_op jit(solution)/shard_map/all_gather | solution.py:116
  63.1 4.6 %all_gather.13 = bf16[32,1024]{1,0:T(8,128)(2,1)S(1)} all-gather(bf16[32,512]{1,0:T(8,128)(2,1)S(1)} %all_to_all.58), channel_id=1, replica_groups=mesh['groups'=2,'row'=4,'col'=2,'sub'=2] {'col'}, dimensions={1}, use_global_device_ids=true | all-gather | bytes 98304 | tf_op jit(solution)/shard_map/all_gather | solution.py:111
  67.7 0.2 reshape.98
  67.9 4.6 %convert_bitcast_fusion = bf16[32,32,32,32]{2,3,0,1:T(8,128)(2,1)} fusion(bf16[32,1,32,32]{3,0,1,2:T(8,128)(2,1)S(1)} %all-gather, bf16[32,32,32]{2,1,0:T(8,128)(2,1)S(1)} %reshape.98), kind=kOutput, calls=%fused_computation | convolution fusion | flops 68157440 | bytes 2228224 | tf_op jit(solution)/shard_map/sic,sje->ijce/dot_general | solution.py:46
  72.4 15.4 %copy.58 = bf16[32,32,32,32]{3,1,2,0:T(8,128)(2,1)} copy(bf16[32,32,32,32]{2,3,0,1:T(8,128)(2,1)} %convert_bitcast_fusion) | data formatting | bytes 4194304 | tf_op jit(solution)/shard_map/convert_element_type | solution.py:48
  87.9 5.4 %fusion.21 = (f32[32,32]{1,0:T(8,128)S(1)}, f32[32,32]{1,0:T(8,128)S(1)}, f32[32,32,128]{2,1,0:T(8,128)S(1)}) fusion(f32[32,32]{1,0:T(8,128)S(1)} %convolution_maximum_fusion, f32[128]{0:T(128)S(1)} %copy-done.4, bf16[32,32,32,32]{3,1,2,0:T(8,128)(2,1)} %copy.58, bf16[32,32,128]{2,1,0:T(8,128)(2,1)S(1)} %copy-done, bf16[32,32,128]{2,1,0:T(8,128)(2,1)S(1)} %copy-done.3), kind=kOutput, calls=%fused_computation.37 | convolution fusion | flops 269350912 | bytes 3158528 | tf_op jit(solution)/shard_map/dot_general | solution.py:50
  93.4 1.0 %add_convert_fusion = bf16[32,32,128]{2,1,0:T(8,128)(2,1)} fusion(f32[32,32,128]{2,1,0:T(8,128)S(1)} %get-tuple-element.15, f32[128]{0:T(128)S(1)} %copy-done.1, f32[128]{0:T(128)S(1)} %copy-done.2, f32[32,32]{1,0:T(8,128)S(1)} %get-tuple-element.12, f32[32,32]{1,0:T(8,128)S(1)} %get-tuple-element.11), kind=kLoop, calls=%fused_computation.20 | loop fusion | flops 655360 | bytes 795648 | tf_op jit(solution)/shard_map/convert_element_type | solution.py:119
  (30 shorter events, 1.2 us)
Async XLA Ops:
  0.0 87.9 %copy-start = (bf16[32,32,128]{2,1,0:T(8,128)(2,1)S(1)}, bf16[32,32,128]{2,1,0:T(8,128)(2,1)}, u32[]{:S(2)}) copy-start(bf16[32,32,128]{2,1,0:T(8,128)(2,1)} %param.24) | copy-start | bytes 786436
  1.5 13.8 %all-to-all-start.3 = ((bf16[4,8,16]{2,0,1:T(4,128)(2,1)}), bf16[4,8,16]{2,0,1:T(4,128)(2,1)S(1)}, u32[]{:S(2)}, u32[]{:S(2)}) async-start(bf16[4,8,16]{2,0,1:T(4,128)(2,1)} %copy.62), calls=%async_computation.3 | async-start | bytes 16384 | tf_op jit(solution)/shard_map/all_to_all | solution.py:103
  15.3 18.5 %all-to-all-start.2 = ((bf16[4,8,16]{2,0,1:T(4,128)(2,1)}), bf16[4,8,16]{2,0,1:T(4,128)(2,1)S(1)}, u32[]{:S(2)}, u32[]{:S(2)}) async-start(bf16[4,8,16]{2,0,1:T(4,128)(2,1)} %copy.59), calls=%async_computation.2 | async-start | bytes 16384 | tf_op jit(solution)/shard_map/all_to_all | solution.py:102
  33.8 10.9 %all-to-all-start = ((bf16[4,8,512]{2,0,1:T(4,128)(2,1)}), bf16[4,8,512]{2,0,1:T(4,128)(2,1)S(1)}, u32[]{:S(2)}, u32[]{:S(2)}) async-start(bf16[4,8,512]{2,0,1:T(4,128)(2,1)} %reshape.110), calls=%async_computation | async-start | bytes 65536 | tf_op jit(solution)/shard_map/all_to_all | solution.py:101
  44.7 18.4 %all-to-all-start.1 = ((bf16[4,8,512]{2,0,1:T(4,128)(2,1)}), bf16[4,8,512]{2,0,1:T(4,128)(2,1)S(1)}, u32[]{:S(2)}, u32[]{:S(2)}) async-start(bf16[4,8,512]{2,0,1:T(4,128)(2,1)} %copy.56), calls=%async_computation.1 | async-start | bytes 65536 | tf_op jit(solution)/shard_map/all_to_all | solution.py:100
  72.4 15.4 %copy-start.3 = (bf16[32,32,128]{2,1,0:T(8,128)(2,1)S(1)}, bf16[32,32,128]{2,1,0:T(8,128)(2,1)}, u32[]{:S(2)}) copy-start(bf16[32,32,128]{2,1,0:T(8,128)(2,1)} %param.17) | copy-start | bytes 786436
  72.4 15.4 %copy-start.4 = (f32[128]{0:T(128)S(1)}, f32[128]{0:T(128)}, u32[]{:S(2)}) copy-start(f32[128]{0:T(128)} %param.25) | copy-start | bytes 1540
  87.9 5.5 %copy-start.1 = (f32[128]{0:T(128)S(1)}, f32[128]{0:T(128)}, u32[]{:S(2)}) copy-start(f32[128]{0:T(128)} %param.27) | copy-start | bytes 1540
  87.9 5.5 %copy-start.2 = (f32[128]{0:T(128)S(1)}, f32[128]{0:T(128)}, u32[]{:S(2)}) copy-start(f32[128]{0:T(128)} %param.26) | copy-start | bytes 1540
where the time goes:
time: 95.2 us; the launch traced here: 94.4 us
  blocking collectives  35.7 us (38%)
  starting transfers between devices  21.2 us (22%)
  local copies, waits for them, and re-layouts  19.4 us (20%)
  matrix products  12.8 us (13%)
  other arithmetic  2.97 us (3%)
  waiting for transfers between devices  2.27 us (2%)
    all_gather x2, blocking collectives, body(): pieces = lax.all_gather((right_part, mask_there), 'row', axis=1, tiled=True)  26.8 us
    convert_element_type x1, local copies, waits for them, and re-layouts, column_terms(): products = jnp.einsum('sic,sje->ijce', left_rows, selected, preferred_ele...  15.4 us
    all_to_all x1, starting transfers between devices, body(): lax.all_to_all(outgoing[3], ('row', 'col'), split_axis=1, concat_axis=0,...  7.25 us
    all_to_all x1, starting transfers between devices, body(): lax.all_to_all(outgoing[2], ('row', 'col'), split_axis=1, concat_axis=0,...  5.88 us
    dot_general x1, matrix products, column_terms(): jnp.dot(products.reshape(pair_rows, -1), out_flat, preferred_element_type...  5.42 us
    all_gather x1, blocking collectives, body(): lax.all_gather(left_part.reshape(sequences, -1), 'col', axis=1, tiled=True)  4.59 us
    dot_general x1, matrix products, column_terms(): jnp.einsum('sic,sje->ijce', left_rows, selected, preferred_element_type=j...  4.58 us
    all_gather x1, blocking collectives, body(): lax.all_gather(mask_here, 'col', axis=1, tiled=True)  4.33 us
  transfers between devices with their start and end apart: 4, of which 2 were waited for; matrix products, arithmetic and copies ran while one was open for 7% of the time, Pallas kernels for 0%

commit v1 on v0

--- a/solution.py
+++ b/solution.py
@@ -1,6 +1,10 @@
+import functools
+
 import jax
 import jax.numpy as jnp
 from jax import lax
+from jax.experimental import pallas as pl
+from jax.experimental.pallas import tpu as pltpu
 from jax.sharding import PartitionSpec as P
 
 
@@ -119,6 +123,202 @@
     return normalize(summed, pair_gain, pair_offset).astype(jnp.bfloat16)
 
 
+F32, BF16 = jnp.float32, jnp.bfloat16
+
+
+def iota(shape, axis):
+    return lax.broadcasted_iota(jnp.int32, shape, axis)
+
+
+def one_hot(condition, kind=BF16):
+    return jnp.where(condition, 1.0, 0.0).astype(kind)
+
+
+def dot(a, b, **options):
+    return jnp.dot(a, b, preferred_element_type=F32, **options)
+
+
+def dot_nt(a, b):
+    return lax.dot_general(a, b, (((1,), (1,)), ((), ())), preferred_element_type=F32)
+
+
+def pair_kernel(
+    row_count, col_count, sub_count,
+    x_ref, am_ref, rm_ref, pair_ref, ag_ref, ao_ref, lw_ref, lo_ref, rw_ref, ro_ref,
+    ow_ref, oo_ref, pg_ref, po_ref, out_ref,
+    send, recv, right_buf, left_wide, w_buf, prod, ml_buf, cm_buf, send_sem, recv_sem,
+):
+    peers = row_count * col_count
+    row, col, sub = lax.axis_index("row"), lax.axis_index("col"), lax.axis_index("sub")
+    me = row * col_count + col
+    barrier = pltpu.get_barrier_semaphore()
+    others = []
+    for k in range(1, peers):
+        peer = lax.rem(me + k, peers)
+        place = {"row": peer // col_count, "col": lax.rem(peer, col_count)}
+        others.append((k, peer, place))
+        pl.semaphore_signal(barrier, inc=1, device_id=place, device_id_type=pl.DeviceIdType.MESH)
+
+    in_32, lane = iota((32, 128), 0), iota((32, 128), 1)
+    rep_left = lane % 32 == in_32
+    rep_right = (lane // 32) * 8 + lane % 8 == in_32
+    wide = jnp.concatenate(
+        [dot(lw_ref[...], one_hot(rep_left)), dot(rw_ref[...], one_hot(rep_right))], axis=1
+    ).astype(BF16)
+    exact = lax.Precision.HIGHEST
+    bias = jnp.concatenate(
+        [
+            dot(jnp.broadcast_to(lo_ref[...], (8, 32)), one_hot(rep_left, F32), precision=exact),
+            dot(jnp.broadcast_to(ro_ref[...], (8, 32)), one_hot(rep_right, F32), precision=exact),
+        ],
+        axis=1,
+    )[0:1]
+    present = (am_ref[...] * rm_ref[...]).astype(F32)
+    at, seq_row = iota((256, 128), 0), None
+    seq_row = jnp.where(at < 128, at // 32, (at // 8) % 4)
+    mask_rows = jnp.zeros((256, 128), F32)
+    for s in range(4):
+        mask_rows = jnp.where(seq_row == s, present[s : s + 1], mask_rows)
+    eye = one_hot(iota((128, 128), 0) == iota((128, 128), 1))
+    mask_here = dot_nt(eye, mask_rows.astype(BF16))
+    lane2 = iota((128, 256), 1)
+    seq_lane = jnp.where(lane2 < 128, lane2 // 32, (lane2 // 8) % 4)
+    sides = jnp.zeros((128, 256), F32)
+    for s in range(4):
+        normed = normalize(x_ref[s].astype(F32), ag_ref[...], ao_ref[...]).astype(BF16)
+        sides = jnp.where(seq_lane == s, dot(normed, wide), sides)
+    sides = ((sides + bias) * mask_here).astype(BF16)
+    left = sides[:, :128]
+    right_buf[...] = sides[:, 128:]
+    mask_block = jnp.concatenate([present, jnp.zeros((12, 128), F32)], axis=0).astype(BF16)
+    for d in range(peers):
+        r, q = d // col_count, d % col_count
+        send[d, 0:32] = left[r * 32 : r * 32 + 32]
+        start = pl.multiple_of((q * sub_count + sub) * 32, 32)
+        send[d, 32:64] = right_buf[pl.ds(start, 32)]
+        send[d, 64:80] = mask_block
+
+    pl.semaphore_wait(barrier, peers - 1)
+    copies = []
+    for k, peer, place in others:
+        copy = pltpu.make_async_remote_copy(
+            src_ref=send.at[peer],
+            dst_ref=recv.at[me],
+            send_sem=send_sem.at[k],
+            recv_sem=recv_sem.at[k],
+            device_id=place,
+            device_id_type=pl.DeviceIdType.MESH,
+        )
+        copy.start()
+        copies.append(copy)
+    recv[me] = send[me]
+
+    for eb in range(4):
+        part = ow_ref[...].astype(F32)[:, eb * 8 : eb * 8 + 8, :]
+        w_buf[eb] = part.reshape(256, 128).astype(BF16)
+    a, b = iota((256, 256), 0), iota((256, 256), 1)
+    swap_rows = one_hot((a % 8 == b // 32) & (a // 8 == b % 32))
+    swap_lanes = one_hot((a // 32 == b % 8) & ((a // 8) % 4 == (b // 8) % 4) & (a % 8 == b // 32))
+    a, b = iota((128, 1024), 0), iota((128, 1024), 1)
+    spread = one_hot((a // 32 == b // 256) & (a % 32 == (b % 256) // 8))
+    a, b = iota((32, 128), 0), iota((32, 128), 1)
+    pick_i = one_hot(a + row * 32 == b)
+    pick_j = one_hot(a + (col * sub_count + sub) * 32 == b)
+    lane_mask = [one_hot(iota((32, 256), 1) % 8 == g) for g in range(8)]
+    ones = jnp.ones((128, 128), BF16)
+
+    for copy in copies:
+        copy.wait()
+
+    got_left = recv[:, 0:32].reshape(256, 128)
+    by_i = dot(swap_rows, got_left).astype(BF16)
+    spread_left = dot(by_i, spread).reshape(32, 8, 1024)
+    left_wide[...] = jnp.concatenate(
+        [spread_left[:, :, s * 256 : s * 256 + 256] for s in range(4)], axis=1
+    ).astype(BF16)
+    got_right = [recv[d, 32:64].astype(F32) for d in range(8)]
+    stacked = jnp.concatenate(
+        [
+            jnp.concatenate([g[:, eb * 32 : eb * 32 + 32] for g in got_right], axis=1)
+            for eb in range(4)
+        ],
+        axis=0,
+    ).astype(BF16)
+    right_rows = dot(stacked, swap_lanes).astype(BF16)
+    masks = recv[:, 64:80].reshape(128, 128)
+    ml_buf[...] = dot_nt(pick_i, masks)
+    mr = dot_nt(pick_j, masks)
+
+    def chunk(step, carry):
+        for n in range(8):
+            i = step * 8 + n
+            base = left_wide[i]
+            block = jnp.concatenate([base * m for m in lane_mask], axis=0)
+            made = dot(right_rows, block).astype(BF16)
+            for eb in range(4):
+                prod[eb, n * 32 : n * 32 + 32] = made[eb * 32 : eb * 32 + 32]
+            cm_buf[n * 32 : n * 32 + 32] = (ml_buf[pl.ds(i, 1)] * mr).astype(BF16)
+        counts = dot(cm_buf[...], ones)
+        total = dot(prod[0], w_buf[0])
+        for eb in range(1, 4):
+            total += dot(prod[eb], w_buf[eb])
+        update = (total + oo_ref[...]) / jnp.maximum(counts, 1.0)
+        first = pl.multiple_of(step * 8, 8)
+        summed = pair_ref[pl.ds(first, 8)].astype(F32).reshape(256, 128) + update
+        result = normalize(summed, pg_ref[...], po_ref[...]).astype(BF16)
+        out_ref[pl.ds(first, 8)] = result.reshape(8, 32, 128)
+        return carry
+
+    lax.fori_loop(0, 4, chunk, 0)
+
+
+def fused_body(
+    alignment, alignment_mask, residue_mask, pair_state, alignment_gain, alignment_offset,
+    left_weight, left_offset, right_weight, right_offset, out_weight, out_offset,
+    pair_gain, pair_offset,
+):
+    row_count = lax.axis_size("row")
+    col_count = lax.axis_size("col")
+    sub_count = lax.axis_size("sub")
+    peers = row_count * col_count
+    vmem = pl.BlockSpec(memory_space=pltpu.VMEM)
+    return pl.pallas_call(
+        functools.partial(pair_kernel, row_count, col_count, sub_count),
+        out_shape=jax.ShapeDtypeStruct(pair_state.shape, BF16),
+        in_specs=[vmem] * 14,
+        out_specs=vmem,
+        scratch_shapes=[
+            pltpu.VMEM((peers, 80, 128), BF16),
+            pltpu.VMEM((peers, 80, 128), BF16),
+            pltpu.VMEM((128, 128), BF16),
+            pltpu.VMEM((32, 32, 256), BF16),
+            pltpu.VMEM((4, 256, 128), BF16),
+            pltpu.VMEM((4, 256, 256), BF16),
+            pltpu.VMEM((32, 128), F32),
+            pltpu.VMEM((256, 128), BF16),
+            pltpu.SemaphoreType.DMA((peers,)),
+            pltpu.SemaphoreType.DMA((peers,)),
+        ],
+        compiler_params=pltpu.CompilerParams(
+            collective_id=0, has_side_effects=True, vmem_limit_bytes=40 * 2**20
+        ),
+    )(
+        alignment, alignment_mask, residue_mask[None], pair_state,
+        alignment_gain[None], alignment_offset[None],
+        left_weight, left_offset[None], right_weight, right_offset[None],
+        out_weight, out_offset[None], pair_gain[None], pair_offset[None],
+    )
+
+
+def fits(alignment, pair_state):
+    senders = lax.axis_size("row") * lax.axis_size("col")
+    return senders == 8 and alignment.shape == (4, 128, 256) and pair_state.shape == (32, 32, 128)
+
+
+def choose(*arrays):
+    return (fused_body if fits(arrays[0], arrays[3]) else body)(*arrays)
+
+
 def solution(mesh):
     placed = (
         P(("groups", "row", "col"), None, None),
@@ -137,7 +337,7 @@
         P(),
     )
     return jax.shard_map(
-        body,
+        choose,
         mesh=mesh,
         in_specs=placed,
         out_specs=P(("groups", "row"), ("col", "sub"), None),

time: 95.2 us -> 17.9 us (0.19)
  blocking collectives: 35.7 us -> 0 us
  starting transfers between devices: 21.2 us -> 0 us
  local copies, waits for them, and re-layouts: 19.4 us -> 5.11 us
  matrix products: 12.8 us -> 0 us
  Pallas kernels: 0 us -> 12.5 us
  other arithmetic: 2.97 us -> 0 us
  waiting for transfers between devices: 2.27 us -> 0 us
    all_gather x4 -> x0, blocking collectives: 35.7 us -> none  [the longest x2 26.8 us: body(): pieces = lax.all_gather((right_part, mask_there), 'row', axis=1, tiled=True)]
    all_to_all x4 -> x0, starting transfers between devices: 21.2 us -> none  [the longest x1 7.25 us: body(): lax.all_to_all(outgoing[3], ('row', 'col'), split_axis=1, concat_axis=0,...]
    convert_element_type x3 -> x0, local copies, waits for them, and re-layouts: 15.7 us -> none  [the longest x1 15.4 us: column_terms(): products = jnp.einsum('sic,sje->ijce', left_rows, selected, preferred_ele...]
    dot_general x5 -> x0, matrix products: 12.8 us -> none  [the longest x1 5.42 us: column_terms(): jnp.dot(products.reshape(pair_rows, -1), out_flat, preferred_element_type...]
    pallas_call x0 -> x1, Pallas kernels: none -> 12.5 us  [fused_body(): pl.pallas_call(functools.partial(pair_kernel, row_count, col_count, sub_c...]
    unnamed x10 -> x29, local copies, waits for them, and re-layouts: 0.02 us -> 5.11 us
    all_to_all x10 -> x0, local copies, waits for them, and re-layouts: 3.05 us -> none  [the longest x3 0.8 us: body(): lax.all_to_all(outgoing[0], ('row', 'col'), split_axis=1, concat_axis=0,...]
    all_to_all x4 -> x0, waiting for transfers between devices: 2.27 us -> none  [the longest x1 2.15 us: body(): lax.all_to_all(outgoing[1], ('row', 'col'), split_axis=1, concat_axis=0,...]
  transfers between devices with their start and end apart: 4 -> 0, of which waited for: 2 -> 0; matrix products, arithmetic and copies ran while one was open for 7% -> 0% of each run, Pallas kernels for 0% -> 0%
where the time goes in v1:
time: 17.9 us; the launch traced here: 17.7 us
  Pallas kernels  12.5 us (70%)
  local copies, waits for them, and re-layouts  5.11 us (29%)
    pallas_call x1, Pallas kernels, fused_body(): pl.pallas_call(functools.partial(pair_kernel, row_count, col_count, sub_c...  12.5 us
    unnamed x29, local copies, waits for them, and re-layouts  5.11 us

profile of v1, /device:TPU:0, one launch (start us, length us, event | category | flops | bytes accessed | tf_op | source)
XLA Modules:
  0.0 17.7 jit_solution(12604129195171519330)
XLA Ops:
  0.0 0.8 %copy.15.lw_ref = bf16[256,32]{1,0:T(8,128)(2,1)S(1)} copy(bf16[256,32]{0,1:T(8,128)(2,1)} %param.20) | data formatting | bytes 32768 | tf_op args[6]
  0.9 0.0 copy-start.3
  0.9 0.0 copy-start.4
  0.9 0.0 copy-start.5
  0.9 0.0 copy-start.6
  0.9 0.0 copy-start.7
  0.9 0.0 copy-start.8
  0.9 0.0 copy-start.9
  0.9 0.0 copy-start.10
  1.0 0.0 copy-start.11
  1.0 0.1 copy.16.rw_ref
  1.1 0.5 %copy-done.3 = s32[4,128]{1,0:T(4,128)S(1)} copy-done((s32[4,128]{1,0:T(4,128)S(1)}, s32[4,128]{1,0:T(4,128)}, u32[]{:S(2)}) %copy-start.3) | copy-done | bytes 2072
  1.5 0.0 copy-done.4
  1.6 0.0 copy-done.5
  1.6 0.0 copy-done.7
  1.6 0.0 copy-done.8
  1.6 0.0 copy-done.9
  1.6 0.0 copy-done.10
  1.6 0.0 copy-done.11
  1.6 0.9 %copy-done = bf16[4,128,256]{2,1,0:T(8,128)(2,1)S(1)} copy-done((bf16[4,128,256]{2,1,0:T(8,128)(2,1)S(1)}, bf16[4,128,256]{2,1,0:T(8,128)(2,1)}, u32[]{:S(2)}) %copy-start) | copy-done | bytes 262168
  2.6 0.9 %copy-done.1 = bf16[32,32,128]{2,1,0:T(8,128)(2,1)S(1)} copy-done((bf16[32,32,128]{2,1,0:T(8,128)(2,1)S(1)}, bf16[32,32,128]{2,1,0:T(8,128)(2,1)}, u32[]{:S(2)}) %copy-start.1) | copy-done | bytes 262168
  3.5 0.9 %copy-done.2 = bf16[32,32,128]{2,1,0:T(8,128)(2,1)S(1)} copy-done((bf16[32,32,128]{2,1,0:T(8,128)(2,1)S(1)}, bf16[32,32,128]{2,1,0:T(8,128)(2,1)}, u32[]{:S(2)}) %copy-start.2) | copy-done | bytes 262168
  4.5 12.5 %shard_map.136 = bf16[32,32,128]{2,1,0:T(8,128)(2,1)S(1)} custom-call(bf16[4,128,256]{2,1,0:T(8,128)(2,1)S(1)} %copy-done, s32[4,128]{1,0:T(4,128)S(1)} %copy-done.3, s32[1,128]{1,0:T(1,128)S(1)} %bitcast.10, bf16[32,32,128]{2,1,0:T(8,128)(2,1)S(1)} %copy-done.1, f32[1,256]{1,0:T(1,128)S(1)} %bitcast.8, f32[1,256]{1,0:T(1,128)S(1)} %bitcast.9, ...), custom_call_target="tpu_custom_call" | custom-call | tf_op jit(solution)/shard_map/pallas_call | solution.py:285
  17.0 0.7 %copy.18 = bf16[32,32,128]{2,1,0:T(8,128)(2,1)} copy(bf16[32,32,128]{2,1,0:T(8,128)(2,1)S(1)} %shard_map.136) | data formatting | bytes 524288
  (6 shorter events, 0.0 us)
Async XLA Ops:
  0.0 0.9 %copy-start.12 = (bf16[256,32]{0,1:T(8,128)(2,1)S(1)}, bf16[256,32]{0,1:T(8,128)(2,1)}, u32[]{:S(2)}) copy-start(bf16[256,32]{0,1:T(8,128)(2,1)} %param.22) | copy-start | bytes 49156
  0.9 0.7 %copy-start.3 = (s32[4,128]{1,0:T(4,128)S(1)}, s32[4,128]{1,0:T(4,128)}, u32[]{:S(2)}) copy-start(s32[4,128]{1,0:T(4,128)} %am_ref.1) | copy-start | bytes 6148
  0.9 0.7 %copy-start.4 = (f32[256]{0:T(256)S(1)}, f32[256]{0:T(256)}, u32[]{:S(2)}) copy-start(f32[256]{0:T(256)} %param.18) | copy-start | bytes 3076
  0.9 0.7 %copy-start.5 = (f32[256]{0:T(256)S(1)}, f32[256]{0:T(256)}, u32[]{:S(2)}) copy-start(f32[256]{0:T(256)} %param.19) | copy-start | bytes 3076
  0.9 0.7 %copy-start.6 = (s32[128]{0:T(128)S(1)}, s32[128]{0:T(128)}, u32[]{:S(2)}) copy-start(s32[128]{0:T(128)} %param.16) | copy-start | bytes 1540
  0.9 0.7 %copy-start.7 = (f32[32]{0:T(128)S(1)}, f32[32]{0:T(128)}, u32[]{:S(2)}) copy-start(f32[32]{0:T(128)} %param.21) | copy-start | bytes 388
  0.9 0.7 %copy-start.8 = (f32[32]{0:T(128)S(1)}, f32[32]{0:T(128)}, u32[]{:S(2)}) copy-start(f32[32]{0:T(128)} %param.23) | copy-start | bytes 388
  0.9 0.7 %copy-start.9 = (f32[128]{0:T(128)S(1)}, f32[128]{0:T(128)}, u32[]{:S(2)}) copy-start(f32[128]{0:T(128)} %param.25) | copy-start | bytes 1540
  0.9 0.7 %copy-start.10 = (f32[128]{0:T(128)S(1)}, f32[128]{0:T(128)}, u32[]{:S(2)}) copy-start(f32[128]{0:T(128)} %param.26) | copy-start | bytes 1540
  1.0 0.7 %copy-start.11 = (f32[128]{0:T(128)S(1)}, f32[128]{0:T(128)}, u32[]{:S(2)}) copy-start(f32[128]{0:T(128)} %param.27) | copy-start | bytes 1540
  1.6 0.9 %copy-start = (bf16[4,128,256]{2,1,0:T(8,128)(2,1)S(1)}, bf16[4,128,256]{2,1,0:T(8,128)(2,1)}, u32[]{:S(2)}) copy-start(bf16[4,128,256]{2,1,0:T(8,128)(2,1)} %x_ref.1) | copy-start | bytes 786436
  2.6 0.9 %copy-start.1 = (bf16[32,32,128]{2,1,0:T(8,128)(2,1)S(1)}, bf16[32,32,128]{2,1,0:T(8,128)(2,1)}, u32[]{:S(2)}) copy-start(bf16[32,32,128]{2,1,0:T(8,128)(2,1)} %pair_ref.1) | copy-start | bytes 786436
  3.5 0.9 %copy-start.2 = (bf16[32,32,128]{2,1,0:T(8,128)(2,1)S(1)}, bf16[32,32,128]{2,1,0:T(8,128)(2,1)}, u32[]{:S(2)}) copy-start(bf16[32,32,128]{2,1,0:T(8,128)(2,1)} %ow_ref.1) | copy-start | bytes 786436

commit v2 on v1

--- a/solution.py
+++ b/solution.py
@@ -142,15 +142,35 @@
     return lax.dot_general(a, b, (((1,), (1,)), ((), ())), preferred_element_type=F32)
 
 
+def dot_tn(a, b):
+    return lax.dot_general(a, b, (((0,), (0,)), ((), ())), preferred_element_type=F32)
+
+
 def pair_kernel(
     row_count, col_count, sub_count,
-    x_ref, am_ref, rm_ref, pair_ref, ag_ref, ao_ref, lw_ref, lo_ref, rw_ref, ro_ref,
-    ow_ref, oo_ref, pg_ref, po_ref, out_ref,
-    send, recv, right_buf, left_wide, w_buf, prod, ml_buf, cm_buf, send_sem, recv_sem,
+    x_hbm, am_hbm, rm_hbm, ag_hbm, ao_hbm, lw_hbm, lo_hbm, rw_hbm, ro_hbm, ow_hbm, pair_hbm,
+    oo_hbm, pg_hbm, po_hbm, out_ref,
+    x_ref, am_ref, rm_ref, ag_ref, ao_ref, lw_ref, lo_ref, rw_ref, ro_ref, ow_ref,
+    pair_ref, oo_ref, pg_ref, po_ref, left_wide, ml_buf, w_buf, prod, cm_buf,
+    send, recv, right_buf, send_sem, recv_sem, load_sem, seq_sem,
 ):
     peers = row_count * col_count
     row, col, sub = lax.axis_index("row"), lax.axis_index("col"), lax.axis_index("sub")
     me = row * col_count + col
+    small = [
+        pltpu.make_async_copy(source, target, load_sem.at[n])
+        for n, (source, target) in enumerate(
+            [
+                (lw_hbm, lw_ref), (rw_hbm, rw_ref), (lo_hbm, lo_ref), (ro_hbm, ro_ref),
+                (am_hbm, am_ref), (rm_hbm, rm_ref), (ag_hbm, ag_ref), (ao_hbm, ao_ref),
+                (ow_hbm, ow_ref), (pair_hbm, pair_ref),
+                (oo_hbm, oo_ref), (pg_hbm, pg_ref), (po_hbm, po_ref),
+            ]
+        )
+    ]
+    seqs = [pltpu.make_async_copy(x_hbm.at[s], x_ref.at[s], seq_sem.at[s]) for s in range(4)]
+    for copy in small[:8] + seqs + small[8:]:
+        copy.start()
     barrier = pltpu.get_barrier_semaphore()
     others = []
     for k in range(1, peers):
@@ -162,10 +182,17 @@
     in_32, lane = iota((32, 128), 0), iota((32, 128), 1)
     rep_left = lane % 32 == in_32
     rep_right = (lane // 32) * 8 + lane % 8 == in_32
+    at = iota((256, 128), 0)
+    seq_row = jnp.where(at < 128, at // 32, (at // 8) % 4)
+    eye = one_hot(iota((128, 128), 0) == iota((128, 128), 1))
+    lane2 = iota((128, 256), 1)
+    seq_lane = jnp.where(lane2 < 128, lane2 // 32, (lane2 // 8) % 4)
+    exact = lax.Precision.HIGHEST
+    for copy in small[:8]:
+        copy.wait()
     wide = jnp.concatenate(
-        [dot(lw_ref[...], one_hot(rep_left)), dot(rw_ref[...], one_hot(rep_right))], axis=1
+        [dot_tn(lw_ref[...], one_hot(rep_left)), dot_tn(rw_ref[...], one_hot(rep_right))], axis=1
     ).astype(BF16)
-    exact = lax.Precision.HIGHEST
     bias = jnp.concatenate(
         [
             dot(jnp.broadcast_to(lo_ref[...], (8, 32)), one_hot(rep_left, F32), precision=exact),
@@ -174,17 +201,13 @@
         axis=1,
     )[0:1]
     present = (am_ref[...] * rm_ref[...]).astype(F32)
-    at, seq_row = iota((256, 128), 0), None
-    seq_row = jnp.where(at < 128, at // 32, (at // 8) % 4)
     mask_rows = jnp.zeros((256, 128), F32)
     for s in range(4):
         mask_rows = jnp.where(seq_row == s, present[s : s + 1], mask_rows)
-    eye = one_hot(iota((128, 128), 0) == iota((128, 128), 1))
     mask_here = dot_nt(eye, mask_rows.astype(BF16))
-    lane2 = iota((128, 256), 1)
-    seq_lane = jnp.where(lane2 < 128, lane2 // 32, (lane2 // 8) % 4)
     sides = jnp.zeros((128, 256), F32)
     for s in range(4):
+        seqs[s].wait()
         normed = normalize(x_ref[s].astype(F32), ag_ref[...], ao_ref[...]).astype(BF16)
         sides = jnp.where(seq_lane == s, dot(normed, wide), sides)
     sides = ((sides + bias) * mask_here).astype(BF16)
@@ -213,6 +236,8 @@
         copies.append(copy)
     recv[me] = send[me]
 
+    for copy in small[8:]:
+        copy.wait()
     for eb in range(4):
         part = ow_ref[...].astype(F32)[:, eb * 8 : eb * 8 + 8, :]
         w_buf[eb] = part.reshape(256, 128).astype(BF16)
@@ -249,27 +274,24 @@
     ml_buf[...] = dot_nt(pick_i, masks)
     mr = dot_nt(pick_j, masks)
 
-    def chunk(step, carry):
+    for step in range(4):
         for n in range(8):
             i = step * 8 + n
             base = left_wide[i]
             block = jnp.concatenate([base * m for m in lane_mask], axis=0)
             made = dot(right_rows, block).astype(BF16)
             for eb in range(4):
-                prod[eb, n * 32 : n * 32 + 32] = made[eb * 32 : eb * 32 + 32]
-            cm_buf[n * 32 : n * 32 + 32] = (ml_buf[pl.ds(i, 1)] * mr).astype(BF16)
-        counts = dot(cm_buf[...], ones)
-        total = dot(prod[0], w_buf[0])
+                prod[step, eb, n * 32 : n * 32 + 32] = made[eb * 32 : eb * 32 + 32]
+            cm_buf[step, n * 32 : n * 32 + 32] = (ml_buf[i : i + 1] * mr).astype(BF16)
+        counts = dot(cm_buf[step], ones)
+        total = dot(prod[step, 0], w_buf[0])
         for eb in range(1, 4):
-            total += dot(prod[eb], w_buf[eb])
+            total += dot(prod[step, eb], w_buf[eb])
         update = (total + oo_ref[...]) / jnp.maximum(counts, 1.0)
-        first = pl.multiple_of(step * 8, 8)
-        summed = pair_ref[pl.ds(first, 8)].astype(F32).reshape(256, 128) + update
+        rows = pl.ds(step * 8, 8)
+        summed = pair_ref[rows].astype(F32).reshape(256, 128) + update
         result = normalize(summed, pg_ref[...], po_ref[...]).astype(BF16)
-        out_ref[pl.ds(first, 8)] = result.reshape(8, 32, 128)
-        return carry
-
-    lax.fori_loop(0, 4, chunk, 0)
+        out_ref[rows] = result.reshape(8, 32, 128)
 
 
 def fused_body(
@@ -282,32 +304,37 @@
     sub_count = lax.axis_size("sub")
     peers = row_count * col_count
     vmem = pl.BlockSpec(memory_space=pltpu.VMEM)
+    hbm = pl.BlockSpec(memory_space=pltpu.HBM)
+    held = (
+        alignment, alignment_mask, residue_mask[None],
+        alignment_gain[None], alignment_offset[None],
+        left_weight.T, left_offset[None], right_weight.T, right_offset[None], out_weight,
+        pair_state, out_offset[None], pair_gain[None], pair_offset[None],
+    )
     return pl.pallas_call(
         functools.partial(pair_kernel, row_count, col_count, sub_count),
         out_shape=jax.ShapeDtypeStruct(pair_state.shape, BF16),
-        in_specs=[vmem] * 14,
+        in_specs=[hbm] * 14,
         out_specs=vmem,
-        scratch_shapes=[
+        scratch_shapes=[pltpu.VMEM(a.shape, a.dtype) for a in held]
+        + [
+            pltpu.VMEM((32, 32, 256), BF16),
+            pltpu.VMEM((32, 128), F32),
+            pltpu.VMEM((4, 256, 128), BF16),
+            pltpu.VMEM((4, 4, 256, 256), BF16),
+            pltpu.VMEM((4, 256, 128), BF16),
             pltpu.VMEM((peers, 80, 128), BF16),
             pltpu.VMEM((peers, 80, 128), BF16),
             pltpu.VMEM((128, 128), BF16),
-            pltpu.VMEM((32, 32, 256), BF16),
-            pltpu.VMEM((4, 256, 128), BF16),
-            pltpu.VMEM((4, 256, 256), BF16),
-            pltpu.VMEM((32, 128), F32),
-            pltpu.VMEM((256, 128), BF16),
             pltpu.SemaphoreType.DMA((peers,)),
             pltpu.SemaphoreType.DMA((peers,)),
+            pltpu.SemaphoreType.DMA((13,)),
+            pltpu.SemaphoreType.DMA((4,)),
         ],
         compiler_params=pltpu.CompilerParams(
             collective_id=0, has_side_effects=True, vmem_limit_bytes=40 * 2**20
         ),
-    )(
-        alignment, alignment_mask, residue_mask[None], pair_state,
-        alignment_gain[None], alignment_offset[None],
-        left_weight, left_offset[None], right_weight, right_offset[None],
-        out_weight, out_offset[None], pair_gain[None], pair_offset[None],
-    )
+    )(*(pltpu.with_memory_space_constraint(a, pltpu.HBM) for a in held))
 
 
 def fits(alignment, pair_state):

time: 17.9 us -> 13.3 us (0.74)
  local copies, waits for them, and re-layouts: 5.11 us -> 0.71 us
  Pallas kernels: 12.5 us -> 12.3 us
    unnamed x29 -> x1, local copies, waits for them, and re-layouts: 5.11 us -> 0.71 us
where the time goes in v2:
time: 13.3 us; the launch traced here: 13 us
  Pallas kernels  12.3 us (92%)
  local copies, waits for them, and re-layouts  0.71 us (5%)
    pallas_call x1, Pallas kernels, fused_body(): pl.pallas_call(functools.partial(pair_kernel, row_count, col_count, sub_c...  12.3 us
    unnamed x1, local copies, waits for them, and re-layouts  0.71 us

profile of v2, /device:TPU:0, one launch (start us, length us, event | category | flops | bytes accessed | tf_op | source)
XLA Modules:
  0.0 13.0 jit_solution(8329291875712204018)
XLA Ops:
  0.0 12.3 %shard_map.136 = bf16[32,32,128]{2,1,0:T(8,128)(2,1)S(1)} custom-call(bf16[4,128,256]{2,1,0:T(8,128)(2,1)} %x_hbm.1, s32[4,128]{1,0:T(4,128)} %am_hbm.1, s32[1,128]{1,0:T(1,128)} %bitcast.14, f32[1,256]{1,0:T(1,128)} %bitcast.12, f32[1,256]{1,0:T(1,128)} %bitcast.13, bf16[32,256]{1,0:T(8,128)(2,1)} %bitcast.10, f32[1,32]{1,0:T(1,128)} %bitcast.15, ...), custom_call_target="tpu_custom_call" | custom-call | tf_op jit(solution)/shard_map/pallas_call | solution.py:314
  12.3 0.7 %copy.16 = bf16[32,32,128]{2,1,0:T(8,128)(2,1)} copy(bf16[32,32,128]{2,1,0:T(8,128)(2,1)S(1)} %shard_map.136) | data formatting | bytes 524288

commit v3 on v2

--- a/solution.py
+++ b/solution.py
@@ -187,19 +187,16 @@
     eye = one_hot(iota((128, 128), 0) == iota((128, 128), 1))
     lane2 = iota((128, 256), 1)
     seq_lane = jnp.where(lane2 < 128, lane2 // 32, (lane2 // 8) % 4)
-    exact = lax.Precision.HIGHEST
-    for copy in small[:8]:
+    for copy in small[:8] + seqs:
         copy.wait()
     wide = jnp.concatenate(
         [dot_tn(lw_ref[...], one_hot(rep_left)), dot_tn(rw_ref[...], one_hot(rep_right))], axis=1
     ).astype(BF16)
     bias = jnp.concatenate(
-        [
-            dot(jnp.broadcast_to(lo_ref[...], (8, 32)), one_hot(rep_left, F32), precision=exact),
-            dot(jnp.broadcast_to(ro_ref[...], (8, 32)), one_hot(rep_right, F32), precision=exact),
-        ],
+        [lo_ref[...]] * 4
+        + [ro_ref[:, eb * 8 : eb * 8 + 8] for eb in range(4) for s in range(4)],
         axis=1,
-    )[0:1]
+    )
     present = (am_ref[...] * rm_ref[...]).astype(F32)
     mask_rows = jnp.zeros((256, 128), F32)
     for s in range(4):
@@ -207,7 +204,6 @@
     mask_here = dot_nt(eye, mask_rows.astype(BF16))
     sides = jnp.zeros((128, 256), F32)
     for s in range(4):
-        seqs[s].wait()
         normed = normalize(x_ref[s].astype(F32), ag_ref[...], ao_ref[...]).astype(BF16)
         sides = jnp.where(seq_lane == s, dot(normed, wide), sides)
     sides = ((sides + bias) * mask_here).astype(BF16)

time: 13.3 us -> 13 us (0.977)
  Pallas kernels: 12.3 us -> 12 us
    pallas_call x1, Pallas kernels: 12.3 us -> 12 us  [fused_body(): pl.pallas_call(functools.partial(pair_kernel, row_count, col_count, sub_c...]
where the time goes in v3:
time: 13 us; the launch traced here: 12.7 us
  Pallas kernels  12 us (92%)
  local copies, waits for them, and re-layouts  0.71 us (5%)
    pallas_call x1, Pallas kernels, fused_body(): pl.pallas_call(functools.partial(pair_kernel, row_count, col_count, sub_c...  12 us
    unnamed x1, local copies, waits for them, and re-layouts  0.71 us

profile of v3, /device:TPU:0, one launch (start us, length us, event | category | flops | bytes accessed | tf_op | source)
XLA Modules:
  0.0 12.7 jit_solution(14699362125128976997)
XLA Ops:
  0.0 12.0 %shard_map.136 = bf16[32,32,128]{2,1,0:T(8,128)(2,1)S(1)} custom-call(bf16[4,128,256]{2,1,0:T(8,128)(2,1)} %x_hbm.1, s32[4,128]{1,0:T(4,128)} %am_hbm.1, s32[1,128]{1,0:T(1,128)} %bitcast.14, f32[1,256]{1,0:T(1,128)} %bitcast.12, f32[1,256]{1,0:T(1,128)} %bitcast.13, bf16[32,256]{1,0:T(8,128)(2,1)} %bitcast.10, f32[1,32]{1,0:T(1,128)} %bitcast.15, ...), custom_call_target="tpu_custom_call" | custom-call | tf_op jit(solution)/shard_map/pallas_call | solution.py:310
  12.0 0.7 %copy.16 = bf16[32,32,128]{2,1,0:T(8,128)(2,1)} copy(bf16[32,32,128]{2,1,0:T(8,128)(2,1)S(1)} %shard_map.136) | data formatting | bytes 524288

commit v4 on v3

--- a/solution.py
+++ b/solution.py
@@ -202,9 +202,18 @@
     for s in range(4):
         mask_rows = jnp.where(seq_row == s, present[s : s + 1], mask_rows)
     mask_here = dot_nt(eye, mask_rows.astype(BF16))
+    all_ones = jnp.ones((256, 128), BF16)
     sides = jnp.zeros((128, 256), F32)
     for s in range(4):
-        normed = normalize(x_ref[s].astype(F32), ag_ref[...], ao_ref[...]).astype(BF16)
+        values = x_ref[s].astype(F32)
+        squares = values * values
+        high = squares.astype(BF16)
+        low = (squares - high.astype(F32)).astype(BF16)
+        average = dot(x_ref[s], all_ones) * (1.0 / 256)
+        scale = (dot(high, all_ones) + dot(low, all_ones)) * (1.0 / 256) - average * average
+        scale = lax.rsqrt(scale + 1e-05)
+        average, scale = (jnp.concatenate([v, v], axis=1) for v in (average, scale))
+        normed = ((values - average) * scale * ag_ref[...] + ao_ref[...]).astype(BF16)
         sides = jnp.where(seq_lane == s, dot(normed, wide), sides)
     sides = ((sides + bias) * mask_here).astype(BF16)
     left = sides[:, :128]

time: 13 us -> 13.3 us (1.023)
  Pallas kernels: 12 us -> 12.4 us
    pallas_call x1, Pallas kernels: 12 us -> 12.4 us  [fused_body(): pl.pallas_call(functools.partial(pair_kernel, row_count, col_count, sub_c...]
where the time goes in v4:
time: 13.3 us; the launch traced here: 13.1 us
  Pallas kernels  12.4 us (93%)
  local copies, waits for them, and re-layouts  0.71 us (5%)
    pallas_call x1, Pallas kernels, fused_body(): pl.pallas_call(functools.partial(pair_kernel, row_count, col_count, sub_c...  12.4 us
    unnamed x1, local copies, waits for them, and re-layouts  0.71 us

profile of v4, /device:TPU:0, one launch (start us, length us, event | category | flops | bytes accessed | tf_op | source)
XLA Modules:
  0.0 13.1 jit_solution(10601559265568795529)
XLA Ops:
  0.0 12.4 %shard_map.136 = bf16[32,32,128]{2,1,0:T(8,128)(2,1)S(1)} custom-call(bf16[4,128,256]{2,1,0:T(8,128)(2,1)} %x_hbm.1, s32[4,128]{1,0:T(4,128)} %am_hbm.1, s32[1,128]{1,0:T(1,128)} %bitcast.14, f32[1,256]{1,0:T(1,128)} %bitcast.12, f32[1,256]{1,0:T(1,128)} %bitcast.13, bf16[32,256]{1,0:T(8,128)(2,1)} %bitcast.10, f32[1,32]{1,0:T(1,128)} %bitcast.15, ...), custom_call_target="tpu_custom_call" | custom-call | tf_op jit(solution)/shard_map/pallas_call | solution.py:319
  12.4 0.7 %copy.16 = bf16[32,32,128]{2,1,0:T(8,128)(2,1)} copy(bf16[32,32,128]{2,1,0:T(8,128)(2,1)S(1)} %shard_map.136) | data formatting | bytes 524288
